TPU v7x, 32 devices: a whole 2x2x4 slice. The times are simulated.
32 devices in a mesh: tok: 4 (over y, x), mem: 4 (over z), row: 2 (over core).
Axes of the slice: x: 2, y: 2, z: 4, core: 2. Of those that a mesh axis runs over, the one named last changes fastest.
Arguments:
- queries: bfloat16 [2, 2048, 8192], P(None, ('tok', 'row'), 'mem'), may hold values from -55 to 55
- keys: bfloat16 [2, 2048, 8192], P(None, ('tok', 'row'), 'mem'), may hold values from -3 to 3
- values: bfloat16 [2, 2048, 8192], P(None, ('tok', 'row'), 'mem'), may hold values from -6 to 6
- token_lr: float32 [16, 2, 2048], P('mem', None, ('tok', 'row')), may hold values from 0.05 to 0.5
- momentum_rate: float32 [16], P('mem'), may hold values from 0.3 to 0.9
- update_step: float32 [16], P('mem'), may hold values from 0.2 to 0.6
- fast_weights: float32 [16, 3, 512, 512], P('mem', None, 'row'), may hold values from -0.25 to 0.25
- momentum: float32 [16, 3, 512, 512], P('mem', None, 'row'), may hold values from -24 to 24
Outputs:
- mixed: bfloat16 [2, 2048, 8192], P(None, ('tok', 'row'), 'mem')
- new_weights: float32 [16, 3, 512, 512], P('mem', None, 'row')
- new_momentum: float32 [16, 3, 512, 512], P('mem', None, 'row')
All inputs are finite; a program needn't handle non-finite values.
Results may differ from a plain program's by a relative error of at most 0.02.
Values may be sent and summed in bfloat16 or wider, within the bound.
No kernel may reach another device: no remote copies, remote signals or barrier semaphores. Data moves between devices by JAX's collectives and lax.ppermute only.
A program may use at most 192 MiB of HBM per device.

v0:
```python
import jax
import jax.numpy as jnp
from jax import lax
from jax.sharding import PartitionSpec as P

DH = 512
HEAD_DIM = 128
WINDOW = 256
NS_STEPS = 2
GROUPS = 2


quintic_one = 3.4445
quintic_two = -4.775
quintic_three = 2.0315


def shifted(value, axis, steps):
    count = lax.axis_size(axis)
    pairs = [(source, (source + steps) % count) for source in range(count)]
    return lax.ppermute(value, axis, pairs)


def unit_rows(field):
    field = field.astype(jnp.float32)
    return field * lax.rsqrt(jnp.mean(field * field, axis=-1, keepdims=True) + 1e-05)


def refine(ortho, gram):
    gram_half = gram.astype(jnp.bfloat16)
    square = jnp.einsum("hmde,hmef->hmdf", gram_half, gram_half, preferred_element_type=jnp.float32)
    poly = (quintic_two * gram + quintic_three * square).astype(jnp.bfloat16)
    turned = jnp.einsum("hmrd,hmde->hmre", ortho, poly, preferred_element_type=jnp.float32)
    return (quintic_one * ortho.astype(jnp.float32) + turned).astype(jnp.bfloat16)


def sliding_attention(queries, keys, values):
    groups, local_len, local_width = queries.shape
    heads = local_width // HEAD_DIM
    tails = jnp.stack([keys, values], axis=0)
    received = shifted(tails, ("tok", "row"), 1)
    device = lax.axis_index(("tok", "row"))
    earlier = jnp.concatenate([jnp.zeros_like(received[:, :1]), received[:, :-1]], axis=1)
    halo = jnp.where(device == 0, earlier, received)
    ext_keys = jnp.concatenate([halo[0], keys], axis=1)
    ext_values = jnp.concatenate([halo[1], values], axis=1)
    block_len = min(local_len, 512)
    count = local_len // block_len
    group_total = local_len * lax.axis_size(("tok", "row"))
    scale = HEAD_DIM ** (-0.5)
    group_base = jnp.arange(groups, dtype=jnp.int32) * group_total + device * local_len

    def attend(block):
        start = block * block_len
        span = block_len + WINDOW
        query_part = queries.reshape(groups, block_len, heads, HEAD_DIM)
        key_part = ext_keys.reshape(groups, span, heads, HEAD_DIM)
        value_part = ext_values.reshape(groups, span, heads, HEAD_DIM)
        scores = (
            jnp.einsum("cqae,ckae->caqk", query_part, key_part, preferred_element_type=jnp.float32)
            * scale
        )
        query_local = start + jnp.arange(block_len, dtype=jnp.int32)
        key_local = start - WINDOW + jnp.arange(span, dtype=jnp.int32)
        offset = query_local[:, None] - key_local[None, :]
        near = (offset >= 0) & (offset < WINDOW)
        placed = group_base[:, None] + key_local[None, :] >= 0
        allowed = near[None, None, :, :] & placed[:, None, None, :]
        scores = jnp.where(allowed, scores, -1e30)
        top = jnp.max(scores, axis=-1, keepdims=True)
        expo = jnp.exp(scores - top)
        probs = (expo / jnp.sum(expo, axis=-1, keepdims=True)).astype(jnp.bfloat16)
        result = jnp.einsum(
            "caqk,ckae->cqae", probs, value_part, preferred_element_type=jnp.float32
        )
        return result.reshape(groups, block_len, local_width)

    pieces = lax.map(attend, jnp.arange(count, dtype=jnp.int32))
    return jnp.moveaxis(pieces, 0, 1).reshape(groups, local_len, local_width)


def shards(queries, keys, values, token_lr, momentum_rate, update_step, fast_weights, momentum):
    attended = sliding_attention(queries, keys, values)
    groups, local_len, local_width = queries.shape
    heads_local = local_width // DH
    query_unit = unit_rows(queries.reshape(groups, local_len, heads_local, DH)).astype(jnp.bfloat16)
    key_unit = unit_rows(keys.reshape(groups, local_len, heads_local, DH)).astype(jnp.bfloat16)
    value_heads = values.reshape(groups, local_len, heads_local, DH)
    rows = fast_weights.shape[2]
    row_start = lax.axis_index("row") * rows
    weights = fast_weights
    moment = momentum
    recalls = []
    for index in range(GROUPS):
        half = lax.all_gather(weights.astype(jnp.bfloat16), "row", axis=2, tiled=True)
        gate_w = half[:, 0]
        up_w = half[:, 1]
        down_w = half[:, 2]
        query_gate = jnp.einsum(
            "lhd,hdf->lhf", query_unit[index], gate_w, preferred_element_type=jnp.float32
        )
        query_up = jnp.einsum(
            "lhd,hdf->lhf", query_unit[index], up_w, preferred_element_type=jnp.float32
        )
        query_hidden = (jax.nn.silu(query_gate) * query_up).astype(jnp.bfloat16)
        recall = jnp.einsum(
            "lhf,hfd->lhd", query_hidden, down_w, preferred_element_type=jnp.float32
        )
        recalls.append(recall.reshape(local_len, local_width))
        key_gate = jnp.einsum(
            "lhd,hdf->lhf", key_unit[index], gate_w, preferred_element_type=jnp.float32
        )
        key_up = jnp.einsum(
            "lhd,hdf->lhf", key_unit[index], up_w, preferred_element_type=jnp.float32
        )
        key_hidden = (jax.nn.silu(key_gate) * key_up).astype(jnp.bfloat16)
        rate = jnp.transpose(token_lr[:, index, :])[:, :, None]
        target = (-(rate * value_heads[index].astype(jnp.float32))).astype(jnp.bfloat16)
        back = jnp.einsum("lhd,hfd->lhf", target, down_w, preferred_element_type=jnp.float32)
        sig = jax.nn.sigmoid(key_gate)
        gate_in = (back * key_up * sig * (1.0 + key_gate * (1.0 - sig))).astype(jnp.bfloat16)
        up_in = (back * jax.nn.silu(key_gate)).astype(jnp.bfloat16)
        gradient = jnp.stack(
            [
                jnp.einsum(
                    "lhd,lhf->hdf", key_unit[index], gate_in, preferred_element_type=jnp.float32
                ),
                jnp.einsum(
                    "lhd,lhf->hdf", key_unit[index], up_in, preferred_element_type=jnp.float32
                ),
                jnp.einsum("lhf,lhd->hfd", key_hidden, target, preferred_element_type=jnp.float32),
            ],
            axis=1,
        )
        halves = lax.psum_scatter(
            gradient.astype(jnp.bfloat16), "row", scatter_dimension=2, tiled=True
        )
        owned = lax.psum(halves, "tok").astype(jnp.float32)
        moment = momentum_rate[:, None, None, None] * moment + owned
        whole = lax.all_gather(moment.astype(jnp.bfloat16), "row", axis=2, tiled=True).astype(
            moment.dtype
        )
        ortho = (
            whole * lax.rsqrt(jnp.sum(whole * whole, axis=(2, 3), keepdims=True) + 1e-06)
        ).astype(jnp.bfloat16)
        for turn in range(NS_STEPS):
            gram = jnp.einsum("hmrd,hmre->hmde", ortho, ortho, preferred_element_type=jnp.float32)
            ortho = refine(ortho, gram)
        ortho = lax.dynamic_slice_in_dim(ortho, row_start, rows, 2)
        stepped = weights - update_step[:, None, None, None] * ortho.astype(jnp.float32)
        columns = lax.psum(jnp.sum(stepped * stepped, axis=2), "row")
        weights = stepped * lax.rsqrt(columns[:, :, None, :] + 1e-06)
    mixed = (attended + jnp.stack(recalls, axis=0)).astype(jnp.bfloat16)
    return (mixed, weights, moment)


def solution(mesh):
    return jax.shard_map(
        shards,
        mesh=mesh,
        in_specs=(
            P(None, ("tok", "row"), "mem"),
            P(None, ("tok", "row"), "mem"),
            P(None, ("tok", "row"), "mem"),
            P("mem", None, ("tok", "row")),
            P("mem"),
            P("mem"),
            P("mem", None, "row", None),
            P("mem", None, "row", None),
        ),
        out_specs=(
            P(None, ("tok", "row"), "mem"),
            P("mem", None, "row", None),
            P("mem", None, "row", None),
        ),
        check_vma=False,
    )
```

profile of v0, /device:TPU:0, one launch (start us, length us, event | category | flops | bytes accessed | tf_op | source)
XLA Modules:
  0.0 618.2 jit_solution(17830953317155994586)
XLA Ops:
  7.2 4.9 copy.192
  18.3 4.1 slice_convert_fusion
  22.4 3.8 reshape.149
  26.7 3.4 multiply_convert_fusion.1
  46.4 15.8 %reduce-scatter.3.cloned.1.call-done = bf16[4,3,256,512]{3,2,0,1:T(8,128)(2,1)} async-done(((bf16[4,3,512,512]{3,2,0,1:T(8,128)(2,1)}), bf16[4,3,256,512]{3,2,0,1:T(8,128)(2,1)}) %reduce-scatter.3.cloned.1.call-update) | async-done | bytes 3145744 | tf_op jit(solution)/shard_map/reduce_scatter | solution.py:135
  62.3 91.7 %all-reduce.4.cloned.1.call-done = bf16[4,3,256,512]{3,2,0,1:T(8,128)(2,1)} async-done(((bf16[4,3,256,512]{3,2,0,1:T(8,128)(2,1)}), bf16[4,3,256,512]{3,2,0,1:T(8,128)(2,1)}) %all-reduce.4.cloned.1.call-update) | async-done | bytes 3145744 | tf_op jit(solution)/shard_map/psum | solution.py:138
  154.0 6.5 %fusion.58 = bf16[4,3,256,512]{3,2,0,1:T(8,128)(2,1)} fusion(bf16[4,3,256,512]{3,2,0,1:T(8,128)(2,1)} %all-reduce.4.cloned.1.call-done, f32[4,3,256,512]{3,2,1,0:T(8,128)} %param.15, f32[4]{0:T(128)S(1)} %copy-done.15), kind=kLoop, calls=%fused_computation.78 | loop fusion | flops 6291456 | bytes 12582928 | tf_op jit(solution)/shard_map/convert_element_type | solution.py:140
  160.6 16.9 %all-gather.7.cloned.1.call-done = bf16[4,3,512,512]{3,2,0,1:T(8,128)(2,1)} async-done(((bf16[4,3,256,512]{3,2,0,1:T(8,128)(2,1)}), bf16[4,3,512,512]{3,2,0,1:T(8,128)(2,1)}) %all-gather.7.cloned.1.call-update) | async-done | bytes 6291472 | tf_op jit(solution)/shard_map/all_gather | solution.py:140
  177.5 4.4 fusion.2
  182.1 7.2 %fusion.18 = f32[4,3,512,512]{3,2,1,0:T(8,128)} fusion(bf16[4,3,512,512]{3,2,0,1:T(8,128)(2,1)S(1)} %copy-done.9, f32[4,3]{0,1:T(4,128)S(1)} %add_rsqrt_fusion.5), kind=kOutput, calls=%fused_computation.35 | convolution fusion | flops 3230662656 | bytes 18874416 | tf_op jit(solution)/shard_map/hmrd,hmre->hmde/dot_general | solution.py:147
  189.3 16.6 %add_convert_fusion.5 = bf16[4,3,512,512]{3,2,1,0:T(8,128)(2,1)} fusion(f32[4,3,512,512]{3,2,1,0:T(8,128)} %fusion.18), kind=kOutput, calls=%fused_computation.18 | convolution fusion | flops 3236954112 | bytes 18874368 | tf_op jit(solution)/shard_map/hmde,hmef->hmdf/dot_general | solution.py:31
  205.9 13.0 %add_convert_fusion.4 = bf16[4,3,512,512]{3,2,0,1:T(8,128)(2,1)} fusion(bf16[4,3,512,512]{3,2,1,0:T(8,128)(2,1)} %add_convert_fusion.5, f32[4,3]{0,1:T(4,128)S(1)} %add_rsqrt_fusion.5, bf16[4,3,512,512]{3,2,0,1:T(8,128)(2,1)} %all-gather.7.cloned.1.call-done), kind=kOutput, calls=%fused_computation.17 | convolution fusion | flops 3252682752 | bytes 18874416 | tf_op jit(solution)/shard_map/hmrd,hmde->hmre/dot_general | solution.py:33
  218.9 12.6 %fusion.16 = f32[4,3,512,512]{3,2,1,0:T(8,128)} fusion(bf16[4,3,512,512]{3,2,0,1:T(8,128)(2,1)} %add_convert_fusion.4), kind=kOutput, calls=%fused_computation.33 | convolution fusion | flops 3221225472 | bytes 18874368 | tf_op jit(solution)/shard_map/hmrd,hmre->hmde/dot_general | solution.py:147
  231.5 17.2 %add_convert_fusion.3 = bf16[4,3,512,512]{3,2,1,0:T(8,128)(2,1)} fusion(f32[4,3,512,512]{3,2,1,0:T(8,128)} %fusion.16), kind=kOutput, calls=%fused_computation.16 | convolution fusion | flops 3236954112 | bytes 18874368 | tf_op jit(solution)/shard_map/hmde,hmef->hmdf/dot_general | solution.py:31
  248.7 12.7 %fusion.24 = f32[4,3,512,512]{3,2,0,1:T(8,128)} fusion(bf16[4,3,512,512]{3,2,0,1:T(8,128)(2,1)} %add_convert_fusion.4, bf16[4,3,512,512]{3,2,1,0:T(8,128)(2,1)} %add_convert_fusion.3), kind=kOutput, calls=%fused_computation.41 | convolution fusion | flops 3221225472 | bytes 25165824 | tf_op jit(solution)/shard_map/hmrd,hmde->hmre/dot_general | solution.py:33
  261.5 7.4 %multiply_reduce_fusion.1 = (f32[4,3,512]{2,0,1:T(4,128)S(1)}, f32[4,3,256,512]{3,2,0,1:T(8,128)}) fusion(f32[4,3,512,512]{3,2,0,1:T(8,128)} %fusion.24, s32[]{:T(128)S(6)} %select_n.20, bf16[4,3,512,512]{3,2,0,1:T(8,128)(2,1)S(1)} %bitcast.257, f32[4]{0:T(128)S(1)} %copy-done.13, f32[4,3,256,512]{3,2,1,0:T(8,128)} %param.14), kind=kLoop, calls=%fused_computation.54 | loop fusion | flops 14149632 | bytes 22044692 | tf_op jit(solution)/shard_map/reduce_sum | solution.py:151
  268.9 3.5 psum.29
  273.0 5.4 multiply_convert_fusion
  278.5 4.0 reshape.150
  282.5 14.2 %all-gather.9.cloned.1.call-done = bf16[4,3,512,512]{3,2,0,1:T(8,128)(2,1)} async-done(((bf16[4,3,256,512]{3,2,0,1:T(8,128)(2,1)}), bf16[4,3,512,512]{3,2,0,1:T(8,128)(2,1)}) %all-gather.9.cloned.1.call-update) | async-done | bytes 6291472 | tf_op jit(solution)/shard_map/all_gather | solution.py:95
  311.3 4.1 copy.55
  315.4 4.4 pad_maximum_fusion.2
  320.0 4.1 copy.62
  331.9 4.5 copy.63
  336.8 3.8 multiply_convert_fusion.2
  340.6 53.6 %collective-permute-done = bf16[2,2,256,2048]{2,3,1,0:T(8,128)(2,1)} collective-permute-done((bf16[2,2,256,2048]{2,3,1,0:T(8,128)(2,1)}, bf16[2,2,256,2048]{2,3,1,0:T(8,128)(2,1)}, u32[]{:S(2)}, u32[]{:S(2)}) %collective-permute-start) | collective-permute-done | bytes 4194336 | tf_op jit(solution)/shard_map/ppermute | solution.py:21
  400.2 11.2 %fusion.52 = f32[2,16,512,256]{3,2,1,0:T(8,128)} fusion(bf16[2,256,16,128]{3,1,2,0:T(8,128)(2,1)} %copy.59, bf16[2,256,16,128]{3,1,2,0:T(8,128)(2,1)} %copy.58, bf16[2,256,2048]{2,1,0:T(8,128)(2,1)} %param.8), kind=kOutput, calls=%fused_computation.66 | convolution fusion | flops 1082130432 | bytes 23068672 | tf_op jit(solution)/shard_map/while/body/eval_jaxpr/cqae,ckae->caqk/dot_general | solution.py:60
  411.4 24.4 %all-reduce.6.cloned.1.call-done = bf16[4,3,256,512]{3,2,0,1:T(8,128)(2,1)} async-done(((bf16[4,3,256,512]{3,2,0,1:T(8,128)(2,1)}), bf16[4,3,256,512]{3,2,0,1:T(8,128)(2,1)}) %all-reduce.6.cloned.1.call-update) | async-done | bytes 3145744 | tf_op jit(solution)/shard_map/psum | solution.py:138
  435.8 6.8 %fusion.132 = (bf16[4,3,256,512]{3,2,0,1:T(8,128)(2,1)}, f32[4,3,256,512]{3,2,0,1:T(8,128)}) fusion(bf16[4,3,256,512]{3,2,0,1:T(8,128)(2,1)} %all-reduce.6.cloned.1.call-done, bf16[4,3,256,512]{3,2,0,1:T(8,128)(2,1)S(1)} %copy-done.4, f32[4,3,256,512]{3,2,1,0:T(8,128)} %param.15, f32[4]{0:T(128)S(1)} %copy-done.15), kind=kLoop, calls=%fused_computation.192 | loop fusion | flops 11010048 | bytes 22020112 | tf_op jit(solution)/shard_map/convert_element_type | solution.py:140
  442.7 22.0 %fusion.135 = (f32[2,16,256]{2,1,0:T(8,128)S(1)}, f32[2,16,256,512]{2,3,1,0:T(8,128)}) fusion(f32[2,16,512,256]{3,2,1,0:T(8,128)} %fusion.52, pred[2,256,512]{1,2,0:T(8,128)(4,1)S(1)} %broadcast_and_fusion), kind=kOutput, calls=%fused_computation.195 | output fusion | flops 25166336 | bytes 33849344 | tf_op jit(solution)/shard_map/while/body/eval_jaxpr/sub | solution.py:71
  464.7 10.6 %fusion.8 = f32[2,16,128,256]{3,2,1,0:T(8,128)} fusion(f32[2,16,256,512]{2,3,1,0:T(8,128)} %get-tuple-element.40, f32[2,16,256]{2,1,0:T(8,128)S(1)} %get-tuple-element.39, bf16[2,256,16,128]{1,3,2,0:T(8,128)(2,1)} %bitcast.264, bf16[2,256,16,128]{1,3,2,0:T(8,128)(2,1)} %bitcast.267), kind=kOutput, calls=%fused_computation.21 | convolution fusion | flops 1090519040 | bytes 25198592 | tf_op jit(solution)/shard_map/while/body/eval_jaxpr/caqk,ckae->cqae/dot_general | solution.py:73
  475.3 3.6 fusion.92
  478.9 5.5 fusion.103
  487.7 3.6 fusion.99
  491.3 5.7 fusion.98
  497.0 3.9 fusion.56
  503.3 6.2 %copy.104 = f32[4,3,256,512]{3,2,1,0:T(8,128)} copy(f32[4,3,256,512]{3,2,0,1:T(8,128)} %get-tuple-element.30) | data formatting | bytes 12582912
  509.5 4.4 fusion.4
  514.1 7.0 %fusion.14 = f32[4,3,512,512]{3,2,1,0:T(8,128)} fusion(bf16[4,3,512,512]{3,2,0,1:T(8,128)(2,1)S(1)} %copy-done.8, f32[4,3]{0,1:T(4,128)S(1)} %add_rsqrt_fusion.4), kind=kOutput, calls=%fused_computation.31 | convolution fusion | flops 3230662656 | bytes 18874416 | tf_op jit(solution)/shard_map/hmrd,hmre->hmde/dot_general | solution.py:147
  521.1 16.8 %add_convert_fusion.2 = bf16[4,3,512,512]{3,2,1,0:T(8,128)(2,1)} fusion(f32[4,3,512,512]{3,2,1,0:T(8,128)} %fusion.14), kind=kOutput, calls=%fused_computation.15 | convolution fusion | flops 3236954112 | bytes 18874368 | tf_op jit(solution)/shard_map/hmde,hmef->hmdf/dot_general | solution.py:31
  537.9 12.9 %add_convert_fusion.1 = bf16[4,3,512,512]{3,2,0,1:T(8,128)(2,1)} fusion(bf16[4,3,512,512]{3,2,1,0:T(8,128)(2,1)} %add_convert_fusion.2, f32[4,3]{0,1:T(4,128)S(1)} %add_rsqrt_fusion.4, bf16[4,3,512,512]{3,2,0,1:T(8,128)(2,1)} %all-gather.11.cloned.1.call-done), kind=kOutput, calls=%fused_computation.14 | convolution fusion | flops 3252682752 | bytes 18874416 | tf_op jit(solution)/shard_map/hmrd,hmde->hmre/dot_general | solution.py:33
  550.7 12.7 %fusion.12 = f32[4,3,512,512]{3,2,1,0:T(8,128)} fusion(bf16[4,3,512,512]{3,2,0,1:T(8,128)(2,1)} %add_convert_fusion.1), kind=kOutput, calls=%fused_computation.29 | convolution fusion | flops 3221225472 | bytes 18874368 | tf_op jit(solution)/shard_map/hmrd,hmre->hmde/dot_general | solution.py:147
  563.4 16.8 %add_convert_fusion = bf16[4,3,512,512]{3,2,1,0:T(8,128)(2,1)} fusion(f32[4,3,512,512]{3,2,1,0:T(8,128)} %fusion.12), kind=kOutput, calls=%fused_computation.13 | convolution fusion | flops 3236954112 | bytes 18874368 | tf_op jit(solution)/shard_map/hmde,hmef->hmdf/dot_general | solution.py:31
  580.1 12.7 %fusion.20 = f32[4,3,512,512]{3,2,0,1:T(8,128)} fusion(bf16[4,3,512,512]{3,2,0,1:T(8,128)(2,1)} %add_convert_fusion.1, bf16[4,3,512,512]{3,2,1,0:T(8,128)(2,1)} %add_convert_fusion), kind=kOutput, calls=%fused_computation.37 | convolution fusion | flops 3221225472 | bytes 25165824 | tf_op jit(solution)/shard_map/hmrd,hmde->hmre/dot_general | solution.py:33
  592.9 6.2 %multiply_reduce_fusion = (f32[4,3,512]{2,0,1:T(4,128)S(1)}, bf16[4,3,256,512]{3,2,0,1:T(8,128)(2,1)}) fusion(f32[4,3,256,512]{3,2,0,1:T(8,128)S(1)} %bitcast.255, f32[4,3,512]{2,0,1:T(4,128)S(1)} %copy-done.11, f32[4]{0:T(128)S(1)} %copy-done.14, f32[4,3,512,512]{3,2,0,1:T(8,128)} %fusion.20, s32[]{:T(128)S(6)} %select_n.20, ...), kind=kLoop, calls=%fused_computation.47 | loop fusion | flops 15722496 | bytes 18923540 | tf_op jit(solution)/shard_map/reduce_sum | solution.py:151
  599.1 3.4 psum.31
  602.5 5.1 fusion.57
  607.6 3.5 copy.103
  (101 shorter events, 58.8 us)
Async XLA Ops:
  7.2 5.0 copy-start.12
  7.2 24.6 %all-gather.5.cloned.1.call-start = ((), (), s32[]{:S(2)}) async-start(), calls=%async_computation.2 | async-start | bytes 9437184 | tf_op jit(solution)/shard_map/all_gather | solution.py:95
  12.1 50.1 %reduce-scatter.3.cloned.1.call-start = ((), (), s32[]{:S(2)}) async-start(), calls=%async_computation.3 | async-start | bytes 9437184 | tf_op jit(solution)/shard_map/reduce_scatter | solution.py:135
  15.1 11.2 %copy-start = (bf16[2,256,2048]{1,2,0:T(8,128)(2,1)}, bf16[2,256,2048]{1,2,0:T(8,128)(2,1)S(1)}, u32[]{:S(2)}) copy-start(bf16[2,256,2048]{1,2,0:T(8,128)(2,1)S(1)} %copy.54) | copy-start | bytes 6291460
  30.1 12.0 %copy-start.2 = (bf16[2,256,4,512]{3,1,2,0:T(8,128)(2,1)}, bf16[2,256,4,512]{3,1,2,0:T(8,128)(2,1)S(1)}, u32[]{:S(2)}) copy-start(bf16[2,256,4,512]{3,1,2,0:T(8,128)(2,1)S(1)} %multiply_convert_fusion.1) | copy-start | bytes 6291460
  31.7 4.8 copy-start.6
  46.3 107.7 %copy-start.15 = (f32[4]{0:T(128)S(1)}, f32[4]{0:T(128)}, u32[]{:S(2)}) copy-start(f32[4]{0:T(128)} %param.12) | copy-start | bytes 52
  46.4 107.6 %all-reduce.4.cloned.1.call-start = ((), (), s32[]{:S(2)}) async-start(), calls=%async_computation.4 | async-start | bytes 6291456 | tf_op jit(solution)/shard_map/psum | solution.py:138
  62.2 115.2 %all-gather.7.cloned.1.call-start = ((), (), s32[]{:S(2)}) async-start(), calls=%async_computation.5 | async-start | bytes 9437184 | tf_op jit(solution)/shard_map/all_gather | solution.py:140
  160.6 136.1 %all-gather.9.cloned.1.call-start = ((), (), s32[]{:S(2)}) async-start(), calls=%async_computation.6 | async-start | bytes 9437184 | tf_op jit(solution)/shard_map/all_gather | solution.py:95
  177.5 4.6 copy-start.9
  231.5 30.0 %slice-start.2 = ((s8[6291456]{0:T(1024)(128)(4,1)}), s8[2097152]{0:T(1024)(128)(4,1)S(1)}, s32[]{:S(2)}) async-start(s8[6291456]{0:T(1024)(128)(4,1)} %bitcast.256), calls=%async_computation.12 | async-start | bytes 4194304
  248.7 12.7 %slice-start.3 = ((s8[6291456]{0:T(1024)(128)(4,1)}), s8[4194304]{0:T(1024)(128)(4,1)S(1)}, s32[]{:S(2)}) async-start(s8[6291456]{0:T(1024)(128)(4,1)} %bitcast.256), calls=%async_computation.13 | async-start | bytes 8388608
  248.7 12.7 %copy-start.13 = (f32[4]{0:T(128)S(1)}, f32[4]{0:T(128)}, u32[]{:S(2)}) copy-start(f32[4]{0:T(128)} %param.13) | copy-start | bytes 52
  272.4 0.6 copy-start.10
  278.4 18.2 %copy-start.3 = (bf16[2,256,4,512]{3,1,2,0:T(8,128)(2,1)S(1)}, bf16[2,256,4,512]{3,1,2,0:T(8,128)(2,1)}, u32[]{:S(2)}) copy-start(bf16[2,256,4,512]{3,1,2,0:T(8,128)(2,1)} %copy-done.2) | copy-start | bytes 6291460
  278.4 50.7 %reduce-scatter.5.cloned.1.call-start = ((), (), s32[]{:S(2)}) async-start(), calls=%async_computation.7 | async-start | bytes 9437184 | tf_op jit(solution)/shard_map/reduce_scatter | solution.py:135
  296.6 4.8 copy-start.7
  311.2 4.1 copy-start.1
  311.2 124.6 %all-reduce.6.cloned.1.call-start = ((), (), s32[]{:S(2)}) async-start(), calls=%async_computation.8 | async-start | bytes 6291456 | tf_op jit(solution)/shard_map/psum | solution.py:138
  319.8 74.4 %collective-permute-start = (bf16[2,2,256,2048]{2,3,1,0:T(8,128)(2,1)}, bf16[2,2,256,2048]{2,3,1,0:T(8,128)(2,1)}, u32[]{:S(2)}, u32[]{:S(2)}) collective-permute-start(bf16[2,2,256,2048]{2,3,1,0:T(8,128)(2,1)} %pad_maximum_fusion.2), channel_id=1, source_target_pairs={{0,1},{1,8},{8,9},{9,16},{16,17},{17,24},{24,25},{25,0},{2,3},{3,1... | collective-permute-start | bytes 12582920 | tf_op jit(solution)/shard_map/ppermute | solution.py:21
  329.2 180.3 %all-gather.11.cloned.1.call-start = ((), (), s32[]{:S(2)}) async-start(), calls=%async_computation.9 | async-start | bytes 9437184 | tf_op jit(solution)/shard_map/all_gather | solution.py:140
  400.2 35.6 %copy-start.4 = (bf16[4,3,256,512]{3,2,0,1:T(8,128)(2,1)S(1)}, bf16[4,3,256,512]{3,2,0,1:T(8,128)(2,1)}, u32[]{:S(2)}) copy-start(bf16[4,3,256,512]{3,2,0,1:T(8,128)(2,1)} %all-reduce.4.cloned.1.call-done) | copy-start | bytes 9437188
  464.7 10.6 %copy-start.5 = (bf16[2,256,4,512]{3,1,2,0:T(8,128)(2,1)S(1)}, bf16[2,256,4,512]{3,1,2,0:T(8,128)(2,1)}, u32[]{:S(2)}) copy-start(bf16[2,256,4,512]{3,1,2,0:T(8,128)(2,1)} %multiply_convert_fusion.2) | copy-start | bytes 6291460
  509.5 4.6 copy-start.8
  563.4 29.5 %slice-start = ((s8[6291456]{0:T(1024)(128)(4,1)}), s8[2097152]{0:T(1024)(128)(4,1)S(1)}, s32[]{:S(2)}) async-start(s8[6291456]{0:T(1024)(128)(4,1)} %bitcast.254), calls=%async_computation.10 | async-start | bytes 4194304
  580.1 12.7 %slice-start.1 = ((s8[6291456]{0:T(1024)(128)(4,1)}), s8[4194304]{0:T(1024)(128)(4,1)S(1)}, s32[]{:S(2)}) async-start(s8[6291456]{0:T(1024)(128)(4,1)} %bitcast.254), calls=%async_computation.11 | async-start | bytes 8388608
  580.1 12.7 %copy-start.11 = (f32[4,3,512]{2,0,1:T(4,128)S(1)}, f32[4,3,512]{2,0,1:T(4,128)}, u32[]{:S(2)}) copy-start(f32[4,3,512]{2,0,1:T(4,128)} %copy-done.10) | copy-start | bytes 73732
  580.1 12.7 %copy-start.14 = (f32[4]{0:T(128)S(1)}, f32[4]{0:T(128)}, u32[]{:S(2)}) copy-start(f32[4]{0:T(128)} %param.13) | copy-start | bytes 52
Sparse Core Ops, SparseCore 0:
  12.2 19.4 all-gather.4
  46.5 15.6 reduce-scatter.2
  65.6 88.3 all-reduce.3
  160.7 16.7 all-gather.6
  278.6 18.0 all-gather.8
  311.4 17.7 reduce-scatter.4
  332.5 103.2 all-reduce.5
  442.8 16.7 all-gather.10
where the time goes:
time: 627 us; the launch traced here: 618 us
  waiting for transfers between devices  221 us (35%)
  matrix products  221 us (35%)
  other arithmetic  97.7 us (16%)
  local copies, waits for them, and re-layouts  56.1 us (9%)
  between operations  14.7 us (2%)
  blocking collectives  6.88 us (1%)
    psum x2, waiting for transfers between devices, shards(): owned = lax.psum(halves, 'tok').astype(jnp.float32)  116 us
    dot_general x4, matrix products, refine(): jnp.einsum('hmde,hmef->hmdf', gram_half, gram_half, preferred_element_typ...  67.3 us
    ppermute x1, waiting for transfers between devices, shifted(): return lax.ppermute(value, axis, pairs)  53.6 us
    dot_general x4, matrix products, refine(): jnp.einsum('hmrd,hmde->hmre', ortho, poly, preferred_element_type=jnp.flo...  51.2 us
    dot_general x4, matrix products, shards(): jnp.einsum('hmrd,hmre->hmde', ortho, ortho, preferred_element_type=jnp.fl...  39.5 us
    unnamed x49, local copies, waits for them, and re-layouts  29.1 us
    sub x1, other arithmetic, attend(): expo = jnp.exp(scores - top)  22 us
    reduce_scatter x2, waiting for transfers between devices, shards(): lax.psum_scatter(gradient.astype(jnp.bfloat16), 'row', scatter_dimension=...  18.7 us
  transfers between devices with their start and end apart: 9, of which 8 were waited for; matrix products, arithmetic and copies ran while one was open for 21% of the time, Pallas kernels for 0%

commit v1 on v0

--- a/solution.py
+++ b/solution.py
@@ -1,6 +1,11 @@
+import functools
+
 import jax
 import jax.numpy as jnp
+import numpy as np
 from jax import lax
+from jax.experimental import pallas as pl
+from jax.experimental.pallas import tpu as pltpu
 from jax.sharding import PartitionSpec as P
 
 DH = 512
@@ -79,7 +84,7 @@
     return jnp.moveaxis(pieces, 0, 1).reshape(groups, local_len, local_width)
 
 
-def shards(queries, keys, values, token_lr, momentum_rate, update_step, fast_weights, momentum):
+def general_shards(queries, keys, values, token_lr, momentum_rate, update_step, fast_weights, momentum):
     attended = sliding_attention(queries, keys, values)
     groups, local_len, local_width = queries.shape
     heads_local = local_width // DH
@@ -154,9 +159,357 @@
     return (mixed, weights, moment)
 
 
+F32 = jnp.float32
+BF16 = jnp.bfloat16
+VMEM_LIMIT = 48 * 1024 * 1024
+
+
+def dot(a, b):
+    return lax.dot_general(a, b, (((1,), (0,)), ((), ())), preferred_element_type=F32)
+
+
+def dot_tn(a, b):
+    return lax.dot_general(a, b, (((0,), (0,)), ((), ())), preferred_element_type=F32)
+
+
+def dot_nt(a, b):
+    return lax.dot_general(a, b, (((1,), (1,)), ((), ())), preferred_element_type=F32)
+
+
+def unit(field):
+    field = field.astype(F32)
+    mean = jnp.mean(field * field, axis=-1, keepdims=True)
+    return (field * lax.rsqrt(mean + 1e-05)).astype(BF16)
+
+
+def sigmoid(value):
+    return 1.0 / (1.0 + jnp.exp(-value))
+
+
+def params(**more):
+    return pltpu.CompilerParams(vmem_limit_bytes=VMEM_LIMIT, **more)
+
+
+def cost(flops, moved):
+    return pl.CostEstimate(flops=int(flops), bytes_accessed=int(moved), transcendentals=0)
+
+
+def prep_body(info, keys, values, rates, *outs):
+    rate_all = rates[0]
+    lanes = lax.broadcasted_iota(jnp.int32, rate_all.shape, 1)
+    width = outs[0].shape[-1]
+    for slot, out in enumerate(outs):
+        head = info[0] ^ slot
+        columns = pl.ds(pl.multiple_of(head * width, width), width)
+        out[0] = unit(keys[0, :, columns])
+        rate = jnp.sum(jnp.where(lanes == head, rate_all, 0.0), axis=1, keepdims=True)
+        out[1] = (-(rate * values[0, :, columns].astype(F32))).astype(BF16)
+
+
+def prep(block, info, keys, values, rates):
+    _, length, width = keys.shape
+    heads = rates.shape[-1]
+    each = jax.ShapeDtypeStruct((2, length, width // heads), BF16)
+    return pl.pallas_call(
+        prep_body,
+        grid_spec=pltpu.PrefetchScalarGridSpec(
+            num_scalar_prefetch=1,
+            grid=(1,),
+            in_specs=[
+                pl.BlockSpec((1, length, width), lambda i, info: (block, 0, 0)),
+                pl.BlockSpec((1, length, width), lambda i, info: (block, 0, 0)),
+                pl.BlockSpec((1, length, heads), lambda i, info: (block, 0, 0)),
+            ],
+            out_specs=[pl.BlockSpec(each.shape, lambda i, info: (0, 0, 0))] * heads,
+        ),
+        out_shape=[each] * heads,
+        compiler_params=params(),
+        cost_estimate=cost(0, 8 * length * width),
+        name="prep",
+    )(info, keys, values, rates)
+
+
+def place_halves(info, target, own, other):
+    rows = own.shape[0]
+    target[pl.ds(pl.multiple_of(info[1] * rows, rows), rows), :] = own.astype(BF16)
+    target[pl.ds(pl.multiple_of((1 - info[1]) * rows, rows), rows), :] = other.astype(BF16)
+
+
+def grad_body(slots, info, *refs):
+    parts = refs[:slots]
+    own, other, out, weights, units, targets, hidden, gates, ups = refs[slots:]
+    length = parts[0].shape[1]
+    for matrix in range(3):
+        place_halves(info, weights.at[matrix], own[0, matrix], other[0, matrix])
+    for slot, part in enumerate(parts):
+        span = pl.ds(slot * length, length)
+        key_unit = part[0]
+        target = part[1]
+        units[span, :] = key_unit
+        targets[span, :] = target
+        key_gate = dot(key_unit, weights[0])
+        key_up = dot(key_unit, weights[1])
+        back = dot_nt(target, weights[2])
+        sig = sigmoid(key_gate)
+        silu = key_gate * sig
+        hidden[span, :] = (silu * key_up).astype(BF16)
+        gates[span, :] = (back * key_up * sig * (1.0 + key_gate * (1.0 - sig))).astype(BF16)
+        ups[span, :] = (back * silu).astype(BF16)
+    rows = own.shape[2]
+    for half in range(2):
+        place = info[1] if half == 0 else 1 - info[1]
+        columns = pl.ds(pl.multiple_of(place * rows, rows), rows)
+        out[half, 0] = dot_tn(units[:, columns], gates[...]).astype(BF16)
+        out[half, 1] = dot_tn(units[:, columns], ups[...]).astype(BF16)
+        out[half, 2] = dot_tn(hidden[:, columns], targets[...]).astype(BF16)
+
+
+def head_spec(shape):
+    alone = shape[0] == 1
+    return pl.BlockSpec((1,) + shape[1:], lambda i, info: (0 if alone else info[0], 0, 0, 0))
+
+
+def grad(info, parts, own, other):
+    slots = len(parts)
+    _, length, width = parts[0].shape
+    rows = own.shape[2]
+    total = slots * length
+    return pl.pallas_call(
+        functools.partial(grad_body, slots),
+        grid_spec=pltpu.PrefetchScalarGridSpec(
+            num_scalar_prefetch=1,
+            grid=(1,),
+            in_specs=[pl.BlockSpec((2, length, width), lambda i, info: (0, 0, 0))] * slots
+            + [head_spec(own.shape)] * 2,
+            out_specs=pl.BlockSpec((2, 3, rows, width), lambda i, info: (0, 0, 0, 0)),
+            scratch_shapes=[pltpu.VMEM((3, width, width), BF16)]
+            + [pltpu.VMEM((total, width), BF16)] * 5,
+        ),
+        out_shape=jax.ShapeDtypeStruct((2, 3, rows, width), BF16),
+        compiler_params=params(),
+        cost_estimate=cost(12 * total * width * width, 4 * total * width + 15 * width * width),
+        name="grad",
+    )(info, *parts, own, other)
+
+
+def polish(ortho):
+    gram = dot_tn(ortho, ortho)
+    gram_half = gram.astype(BF16)
+    square = dot(gram_half, gram_half)
+    poly = (quintic_two * gram + quintic_three * square).astype(BF16)
+    return (quintic_one * ortho.astype(F32) + dot(ortho, poly)).astype(BF16)
+
+
+def update_body(summed, last, kept, info, rate, step, ga, gb, m_own, m_oth, w_own, w_oth, *refs):
+    refs = refs[kept:]
+    if last:
+        m_out, w_out = refs[:2]
+        refs = refs[2:]
+    else:
+        m_out, mo_out, w_out, wo_out = refs[:4]
+        refs = refs[4:]
+    head = info[0]
+    alone = []
+    if summed:
+        g_out, *alone, g_own, g_oth = refs
+        g_own[...] = (ga[0, 0].astype(F32) + gb[1, 0].astype(F32)).astype(BF16)
+        g_oth[...] = (ga[1, 0].astype(F32) + gb[0, 0].astype(F32)).astype(BF16)
+        g_out[0] = g_own[...]
+        grad_own = g_own[...].astype(F32)
+        grad_oth = g_oth[...].astype(F32)
+    else:
+        grad_own = ga[0].astype(F32)
+        grad_oth = gb[0].astype(F32)
+    moment_own = rate[head] * m_own[0, 0] + grad_own
+    moment_oth = rate[head] * m_oth[0, 0] + grad_oth
+    m_out[0, 0] = moment_own
+    if not last:
+        mo_out[0, 0] = moment_oth
+    power = jnp.sum(moment_own * moment_own + moment_oth * moment_oth, keepdims=True)
+    scale = lax.rsqrt(power + 1e-06)
+    ortho = jnp.concatenate(
+        [(moment_own * scale).astype(BF16), (moment_oth * scale).astype(BF16)], axis=0
+    )
+    for turn in range(NS_STEPS):
+        ortho = polish(ortho)
+    rows = m_own.shape[2]
+    stepped_own = w_own[0, 0] - step[head] * ortho[:rows].astype(F32)
+    stepped_oth = w_oth[0, 0] - step[head] * ortho[rows:].astype(F32)
+    columns = jnp.sum(stepped_own * stepped_own + stepped_oth * stepped_oth, axis=0, keepdims=True)
+    scale = lax.rsqrt(columns + 1e-06)
+    w_out[0, 0] = stepped_own * scale
+    if not last:
+        wo_out[0, 0] = stepped_oth * scale
+    if alone:
+        alone[0][0, 0] = moment_own
+        alone[1][0, 0] = moment_oth
+        alone[2][0, 0] = stepped_own * scale
+        alone[3][0, 0] = stepped_oth * scale
+
+
+def update(info, rate, step, ga, gb, state, previous, summed, last):
+    _, _, rows, width = state[0].shape
+    heads = rate.shape[0]
+    block = pl.BlockSpec((1, 1, rows, width), lambda m, info: (info[0], m, 0, 0))
+    alone = pl.BlockSpec((1, 1, rows, width), lambda m, info: (0, m, 0, 0))
+    scalars = pl.BlockSpec(memory_space=pltpu.SMEM)
+    if summed:
+        g_spec = pl.BlockSpec((2, 1, rows, width), lambda m, info: (0, m, 0, 0))
+    else:
+        g_spec = pl.BlockSpec((1, rows, width), lambda m, info: (m, 0, 0))
+    whole = jax.ShapeDtypeStruct((heads, 3, rows, width), F32)
+    count = 2 if last else 4
+    out_shape = [whole] * count
+    out_specs = [block] * count
+    scratch = []
+    if summed:
+        out_shape.append(jax.ShapeDtypeStruct((3, rows, width), BF16))
+        out_specs.append(pl.BlockSpec((1, rows, width), lambda m, info: (m, 0, 0)))
+        if not last:
+            out_shape += [jax.ShapeDtypeStruct((1, 3, rows, width), F32)] * 4
+            out_specs += [alone] * 4
+        scratch = [pltpu.VMEM((rows, width), BF16)] * 2
+    kept = 0 if previous is None else count
+    return pl.pallas_call(
+        functools.partial(update_body, summed, last, kept),
+        grid_spec=pltpu.PrefetchScalarGridSpec(
+            num_scalar_prefetch=1,
+            grid=(3,),
+            in_specs=[scalars] * 2 + [g_spec] * 2
+            + [block if value.shape[0] == heads else alone for value in state]
+            + [pl.BlockSpec(memory_space=pl.ANY)] * kept,
+            out_specs=out_specs,
+            scratch_shapes=scratch,
+        ),
+        out_shape=out_shape,
+        input_output_aliases={9 + i: i for i in range(kept)},
+        compiler_params=params(),
+        cost_estimate=cost(3 * 6 * 2 * width**3, 3 * 16 * rows * width),
+        name="update",
+    )(info, rate, step, ga, gb, *state, *(previous or []))
+
+
+def mix_body(block, kept, info, queries, keys, values, early_k, early_v, own, other, *refs):
+    out, weights = refs[kept:]
+    length, width = queries.shape[1:]
+    for matrix in range(3):
+        place_halves(info, weights.at[matrix], own[0, matrix], other[0, matrix])
+    query_unit = unit(queries[0])
+    gate = dot(query_unit, weights[0])
+    hidden = (gate * sigmoid(gate) * dot(query_unit, weights[1])).astype(BF16)
+    recall = dot(hidden, weights[2])
+    rows = lax.broadcasted_iota(jnp.int32, (length, length), 0)
+    lanes = lax.broadcasted_iota(jnp.int32, (length, length), 1)
+    here = lanes <= rows
+    factor = HEAD_DIM ** (-0.5) * float(np.log2(np.e))
+    for head in range(width // HEAD_DIM):
+        columns = slice(head * HEAD_DIM, (head + 1) * HEAD_DIM)
+        query = queries[0, :, columns]
+        late = dot_nt(query, keys[0, :, columns])
+        early = dot_nt(query, early_k[0, :, columns])
+        if block == 0:
+            early = early + jnp.where(info[2] == 1, -1e30, 0.0)
+        scores = jnp.where(here, late, early)
+        top = jnp.max(scores, axis=1, keepdims=True)
+        expo = jnp.exp2((scores - top) * factor)
+        total = jnp.sum(expo, axis=1, keepdims=True)
+        result = dot(jnp.where(here, expo, 0.0).astype(BF16), values[0, :, columns])
+        result += dot(jnp.where(here, 0.0, expo).astype(BF16), early_v[0, :, columns])
+        out[0, :, columns] = (result * (1.0 / total) + recall[:, columns]).astype(BF16)
+
+
+def mix(block, info, queries, keys, values, early_k, early_v, own, other, previous):
+    groups, length, width = queries.shape
+    heads = own.shape[0]
+    part = width // heads
+    here = pl.BlockSpec((1, length, part), lambda h, info: (block, 0, h))
+    if block:
+        before = pl.BlockSpec((1, length, part), lambda h, info: (block - info[2], 0, h))
+    else:
+        before = here
+    weight = pl.BlockSpec((1,) + own.shape[1:], lambda h, info: (h, 0, 0, 0))
+    kept = [] if previous is None else [previous]
+    return pl.pallas_call(
+        functools.partial(mix_body, block, len(kept)),
+        grid_spec=pltpu.PrefetchScalarGridSpec(
+            num_scalar_prefetch=1,
+            grid=(heads,),
+            in_specs=[here] * 3 + [before] * 2 + [weight] * 2
+            + [pl.BlockSpec(memory_space=pl.ANY)] * len(kept),
+            out_specs=here,
+            scratch_shapes=[pltpu.VMEM((3, part, part), BF16)],
+        ),
+        out_shape=jax.ShapeDtypeStruct(queries.shape, BF16),
+        input_output_aliases={8: 0} if kept else {},
+        compiler_params=params(),
+        cost_estimate=cost(
+            heads * (6 * length * part * part + 8 * length * length * part),
+            12 * length * width + 12 * width * part,
+        ),
+        name="mix",
+    )(info, queries, keys, values, early_k, early_v, own, other, *kept)
+
+
+def owner_shards(queries, keys, values, token_lr, momentum_rate, update_step, fast_weights, momentum):
+    groups, length, _ = queries.shape
+    chips = lax.axis_size("tok")
+    chip = lax.axis_index("tok")
+    row = lax.axis_index("row")
+    first = (lax.axis_index(("tok", "row")) == 0).astype(jnp.int32)
+    infos = [jnp.stack([chip ^ slot, row, first]).astype(jnp.int32) for slot in range(chips)]
+    rates = jnp.transpose(token_lr, (1, 2, 0))
+
+    def to_chip(value, slot):
+        return lax.ppermute(value, "tok", [(c, c ^ slot) for c in range(chips)])
+
+    def to_core(value):
+        return lax.ppermute(value, "row", [(0, 1), (1, 0)])
+
+    early_k = shifted(keys, ("tok", "row"), 1)
+    early_v = shifted(values, ("tok", "row"), 1)
+    w_own, m_own = fast_weights, momentum
+    w_oth, m_oth = to_core(fast_weights), to_core(momentum)
+    parts = []
+    for block in range(groups):
+        sent = prep(block, infos[0], keys, values, rates)
+        parts.append([sent[0]] + [to_chip(sent[slot], slot) for slot in range(1, chips)])
+    mixed = None
+    alone = (m_own, m_oth, w_own, w_oth)
+    for block in range(groups):
+        last = block == groups - 1
+        partial = grad(infos[0], parts[block], alone[2], alone[3])
+        state = (m_own, m_oth, w_own, w_oth)
+        results = update(
+            infos[0], momentum_rate, update_step, partial, to_core(partial), alone, None, True, last
+        )
+        count = 2 if last else 4
+        after, gradient, alone = results[:count], results[count], results[count + 1 :]
+        mixed = mix(
+            block, infos[0], queries, keys, values, early_k, early_v, w_own, w_oth, mixed
+        )
+        for slot in range(1, chips):
+            arrived = to_chip(gradient, slot)
+            after = update(
+                infos[slot], momentum_rate, update_step, arrived, to_core(arrived), state, after,
+                False, last,
+            )
+        if last:
+            m_own, w_own = after
+        else:
+            m_own, m_oth, w_own, w_oth = after
+    return (mixed, w_own, m_own)
+
+
+def shards(chips, queries, *rest):
+    heads = queries.shape[2] // DH
+    if heads == chips and chips & (chips - 1) == 0 and queries.shape[1] == WINDOW:
+        return owner_shards(queries, *rest)
+    return general_shards(queries, *rest)
+
+
 def solution(mesh):
     return jax.shard_map(
-        shards,
+        functools.partial(shards, mesh.shape["tok"]),
         mesh=mesh,
         in_specs=(
             P(None, ("tok", "row"), "mem"),

time: 627 us -> 267 us (0.43); the launches traced: 618 us -> 267 us
  matrix products: 221 us -> 0 us
  Pallas kernels: 0 us -> 140 us
  waiting for transfers between devices: 221 us -> 101 us
  other arithmetic: 97.7 us -> 0.3 us
  local copies, waits for them, and re-layouts: 56.1 us -> 7.34 us
  starting transfers between devices: 0.52 us -> 17.7 us
  between operations: 14.7 us -> 0.8 us
  blocking collectives: 6.88 us -> 0 us
    dot_general x30 -> x0, matrix products: 221 us -> none  [the longest x4 67.3 us: refine(): jnp.einsum('hmde,hmef->hmdf', gram_half, gram_half, preferred_element_typ...]
    pallas_call x0 -> x14, Pallas kernels: none -> 140 us  [the longest x8 96.6 us: update(): pl.pallas_call(functools.partial(update_body, summed, last, kept), grid_s...]
    psum x2 -> x0, waiting for transfers between devices: 116 us -> none  [shards(): owned = lax.psum(halves, 'tok').astype(jnp.float32)]
    ppermute x0 -> x22, waiting for transfers between devices: none -> 101 us  [the longest x12 101 us: to_chip(): return lax.ppermute(value, 'tok', [(c, c ^ slot) for c in range(chips)])]
    ppermute x1 -> x2, waiting for transfers between devices: 53.6 us -> 0.01 us  [shifted(): return lax.ppermute(value, axis, pairs)]
    convert_element_type x7 -> x0, other arithmetic: 34.1 us -> none  [the longest x2 13.4 us: shards(): moment.astype(jnp.bfloat16)]
    all_gather x4 -> x0, waiting for transfers between devices: 32.6 us -> none  [the longest x2 16.9 us: shards(): lax.all_gather(moment.astype(jnp.bfloat16), 'row', axis=2, tiled=True)]
    reduce_sum x6 -> x0, other arithmetic: 25 us -> none  [the longest x2 13.7 us: shards(): columns = lax.psum(jnp.sum(stepped * stepped, axis=2), 'row')]
  transfers between devices with their start and end apart: 9 -> 24, of which waited for: 8 -> 5; matrix products, arithmetic and copies ran while one was open for 21% -> 0% of each run, Pallas kernels for 0% -> 48%
where the time goes in v1:
time: 267 us
  Pallas kernels  140 us (52%)
  waiting for transfers between devices  101 us (38%)
  starting transfers between devices  17.7 us (7%)
  local copies, waits for them, and re-layouts  7.34 us (3%)
    ppermute x12, waiting for transfers between devices, to_chip(): return lax.ppermute(value, 'tok', [(c, c ^ slot) for c in range(chips)])  101 us
    pallas_call x8, Pallas kernels, update(): pl.pallas_call(functools.partial(update_body, summed, last, kept), grid_s...  96.6 us
    pallas_call x2, Pallas kernels, mix(): pl.pallas_call(functools.partial(mix_body, block, len(kept)), grid_spec=p...  24.2 us
    ppermute x12, starting transfers between devices, to_chip(): return lax.ppermute(value, 'tok', [(c, c ^ slot) for c in range(chips)])  14.9 us
    pallas_call x2, Pallas kernels, grad(): pl.pallas_call(functools.partial(grad_body, slots), grid_spec=pltpu.Prefe...  14.5 us
    unnamed x23, local copies, waits for them, and re-layouts  7.34 us
  transfers between devices with their start and end apart: 24, of which 5 were waited for; matrix products, arithmetic and copies ran while one was open for 0% of the time, Pallas kernels for 48%

profile of v1, /device:TPU:0, one launch (start us, length us, event | category | flops | bytes accessed | tf_op | source)
XLA Modules:
  0.0 266.9 jit_solution(15827413997073723460)
XLA Ops:
  0.6 0.5 collective-permute-start.5
  1.1 0.1 collective-permute-start.7
  1.2 0.8 copy.30
  2.1 0.1 add_add_fusion.info
  2.2 1.6 copy-done
  3.7 2.4 prep.2
  6.1 3.0 %collective-permute-start.2 = (bf16[2,256,512]{2,1,0:T(8,128)(2,1)S(1)}, bf16[2,256,512]{2,1,0:T(8,128)(2,1)S(1)}, u32[]{:S(2)}, u32[]{:S(2)}) collective-permute-start(bf16[2,256,512]{2,1,0:T(8,128)(2,1)S(1)} %get-tuple-element.42), channel_id=1, source_target_pairs={{0,8},{8,0},{16,24},{24,16},{1,9},{9,1},{17,25},{25,17},{2,10},{10... | collective-permute-start | bytes 1572872 | tf_op jit(solution)/shard_map/ppermute | solution.py:463
  9.1 1.5 collective-permute-start.3
  10.6 0.0 collective-permute-start.4
  10.7 11.2 %collective-permute-done.2.refs_1_ = bf16[2,256,512]{2,1,0:T(8,128)(2,1)S(1)} collective-permute-done((bf16[2,256,512]{2,1,0:T(8,128)(2,1)S(1)}, bf16[2,256,512]{2,1,0:T(8,128)(2,1)S(1)}, u32[]{:S(2)}, u32[]{:S(2)}) %collective-permute-start.2) | collective-permute-done | bytes 524320 | tf_op jit(solution)/shard_map/ppermute | solution.py:463
  21.8 12.1 %collective-permute-done.3.refs_2_ = bf16[2,256,512]{2,1,0:T(8,128)(2,1)S(1)} collective-permute-done((bf16[2,256,512]{2,1,0:T(8,128)(2,1)S(1)}, bf16[2,256,512]{2,1,0:T(8,128)(2,1)S(1)}, u32[]{:S(2)}, u32[]{:S(2)}) %collective-permute-start.3) | collective-permute-done | bytes 524320 | tf_op jit(solution)/shard_map/ppermute | solution.py:463
  34.0 7.0 %grad.2.ga = bf16[2,3,256,512]{3,2,1,0:T(8,128)(2,1)S(1)} custom-call(s32[3]{0:T(128)S(1)} %add_add_fusion.info, bf16[2,256,512]{2,1,0:T(8,128)(2,1)S(1)} %get-tuple-element.41.refs_0_, bf16[2,256,512]{2,1,0:T(8,128)(2,1)S(1)} %collective-permute-done.2.refs_1_, bf16[2,256,512]{2,1,0:T(8,128)(2,1)S(1)} %collective-permute-done.3.refs_2_, ...), custom_call_target="tpu_custom_call" | custom-call | flops 3221225472 | bytes 6029312 | tf_op jit(solution)/shard_map/grad/pallas_call | solution.py:277
  41.0 0.0 copy-start.3
  41.0 0.1 collective-permute-start.6
  41.1 2.4 prep.3
  43.5 1.3 collective-permute-start.14
  44.8 0.8 collective-permute-start.15
  45.6 1.4 collective-permute-start.16
  47.1 0.0 copy-start.10
  47.1 1.1 copy-done.10
  48.2 13.8 %update.8 = (f32[4,3,256,512]{3,2,1,0:T(8,128)}, f32[4,3,256,512]{3,2,1,0:T(8,128)}, f32[4,3,256,512]{3,2,1,0:T(8,128)}, f32[4,3,256,512]{3,2,1,0:T(8,128)}, bf1...) custom-call(s32[3]{0:T(128)S(1)} %add_add_fusion.info, ...), custom_call_target="tpu_custom_call" | custom-call | flops 4831838208 | bytes 6291456 | tf_op jit(solution)/shard_map/update/pallas_call | solution.py:373
  62.0 1.1 copy-done.6
  63.2 1.2 copy-done.8
  64.4 26.5 %collective-permute-done.15.refs_2_ = bf16[2,256,512]{2,1,0:T(8,128)(2,1)S(1)} collective-permute-done((bf16[2,256,512]{2,1,0:T(8,128)(2,1)S(1)}, bf16[2,256,512]{2,1,0:T(8,128)(2,1)S(1)}, u32[]{:S(2)}, u32[]{:S(2)}) %collective-permute-start.15) | collective-permute-done | bytes 524320 | tf_op jit(solution)/shard_map/ppermute | solution.py:463
  90.9 7.5 %grad.3.ga = bf16[2,3,256,512]{3,2,1,0:T(8,128)(2,1)} custom-call(s32[3]{0:T(128)S(1)} %add_add_fusion.info, bf16[2,256,512]{2,1,0:T(8,128)(2,1)S(1)} %get-tuple-element.60.refs_0_, bf16[2,256,512]{2,1,0:T(8,128)(2,1)S(1)} %collective-permute-done.14.refs_1_, bf16[2,256,512]{2,1,0:T(8,128)(2,1)S(1)} %collective-permute-done.15.refs_2_, ...), custom_call_target="tpu_custom_call" | custom-call | flops 3221225472 | bytes 6029312 | tf_op jit(solution)/shard_map/grad/pallas_call | solution.py:277
  98.4 0.5 collective-permute-start.1
  98.9 2.5 collective-permute-start.10
  101.4 0.1 add_add_fusion.1.info
  101.5 0.1 add_add_fusion.2.info
  101.5 40.2 %collective-permute-done.10.ga = bf16[3,256,512]{2,1,0:T(8,128)(2,1)S(1)} collective-permute-done((bf16[3,256,512]{2,1,0:T(8,128)(2,1)}, bf16[3,256,512]{2,1,0:T(8,128)(2,1)S(1)}, u32[]{:S(2)}, u32[]{:S(2)}) %collective-permute-start.10) | collective-permute-done | bytes 786464 | tf_op jit(solution)/shard_map/ppermute | solution.py:463
  141.8 1.0 collective-permute-start.11
  142.8 1.4 copy-done.7
  144.2 12.1 %update.12 = (f32[4,3,256,512]{3,2,1,0:T(8,128)}, f32[4,3,256,512]{3,2,1,0:T(8,128)}, bf16[3,256,512]{2,1,0:T(8,128)(2,1)S(1)}) custom-call(s32[3]{0:T(128)S(1)} %add_add_fusion.info, f32[4]{0:T(128)S(1)} %copy-done.4, f32[4]{0:T(128)S(1)} %copy-done.5, bf16[2,3,256,512]{3,2,1,0:T(8,128)(2,1)} %grad.3.ga, ...), custom_call_target="tpu_custom_call" | custom-call | flops 4831838208 | bytes 6291456 | tf_op jit(solution)/shard_map/update/pallas_call | solution.py:373
  156.3 2.8 %collective-permute-start.22 = (bf16[3,256,512]{2,1,0:T(8,128)(2,1)S(1)}, bf16[3,256,512]{2,1,0:T(8,128)(2,1)S(1)}, u32[]{:S(2)}, u32[]{:S(2)}) collective-permute-start(bf16[3,256,512]{2,1,0:T(8,128)(2,1)S(1)} %get-tuple-element.68), channel_id=1, source_target_pairs={{0,8},{8,0},{16,24},{24,16},{1,9},{9,1},{17,25},{25,17},{2,10},{10... | collective-permute-start | bytes 2359304 | tf_op jit(solution)/shard_map/ppermute | solution.py:463
  159.1 0.1 add_add_fusion.3.info
  159.2 11.9 %mix.2.refs_0_ = bf16[2,256,2048]{2,1,0:T(8,128)(2,1)} custom-call(s32[3]{0:T(128)S(1)} %add_add_fusion.info, bf16[2,256,2048]{2,1,0:T(8,128)(2,1)S(1)} %copy-done.2, bf16[2,256,2048]{2,1,0:T(8,128)(2,1)S(1)} %copy-done.1, bf16[2,256,2048]{2,1,0:T(8,128)(2,1)} %values.7, bf16[2,256,2048]{2,1,0:T(8,128)(2,1)} %collective-permute-done.early_k, ...), custom_call_target="tpu_custom_call" | custom-call | flops 2684354560 | bytes 18874368 | tf_op jit(solution)/shard_map/mix/pallas_call | solution.py:432
  171.1 0.1 collective-permute-start.18
  171.2 1.5 collective-permute-start.20
  172.7 12.2 %update.9 = (f32[4,3,256,512]{3,2,1,0:T(8,128)}, f32[4,3,256,512]{3,2,1,0:T(8,128)}, f32[4,3,256,512]{3,2,1,0:T(8,128)}, f32[4,3,256,512]{3,2,1,0:T(8,128)}) custom-call(s32[3]{0:T(128)S(1)} %add_add_fusion.3.info, f32[4]{0:T(128)S(1)} %copy-done.4, f32[4]{0:T(128)S(1)} %copy-done.5, ...), custom_call_target="tpu_custom_call", output_to_operand_aliasing={{0}: (9, {}), {1}: (10, {}), {2}: (11, {}), {3}: (12, {})} | custom-call | flops 4831838208 | bytes 6291456 | tf_op jit(solution)/shard_map/update/pallas_call | solution.py:373
  184.9 0.1 collective-permute-start.23
  185.0 12.2 %update.10 = (f32[4,3,256,512]{3,2,1,0:T(8,128)}, f32[4,3,256,512]{3,2,1,0:T(8,128)}, f32[4,3,256,512]{3,2,1,0:T(8,128)}, f32[4,3,256,512]{3,2,1,0:T(8,128)}) custom-call(s32[3]{0:T(128)S(1)} %add_add_fusion.2.info, f32[4]{0:T(128)S(1)} %copy-done.4, f32[4]{0:T(128)S(1)} %copy-done.5, ...), custom_call_target="tpu_custom_call", output_to_operand_aliasing={{0}: (9, {}), {1}: (10, {}), {2}: (11, {}), {3}: (12, {})} | custom-call | flops 4831838208 | bytes 6291456 | tf_op jit(solution)/shard_map/update/pallas_call | solution.py:373
  197.2 10.7 %collective-permute-done.20.ga = bf16[3,256,512]{2,1,0:T(8,128)(2,1)S(1)} collective-permute-done((bf16[3,256,512]{2,1,0:T(8,128)(2,1)S(1)}, bf16[3,256,512]{2,1,0:T(8,128)(2,1)S(1)}, u32[]{:S(2)}, u32[]{:S(2)}) %collective-permute-start.20) | collective-permute-done | bytes 786464 | tf_op jit(solution)/shard_map/ppermute | solution.py:463
  207.9 12.1 %update.11 = (f32[4,3,256,512]{3,2,1,0:T(8,128)}, f32[4,3,256,512]{3,2,1,0:T(8,128)}, f32[4,3,256,512]{3,2,1,0:T(8,128)}, f32[4,3,256,512]{3,2,1,0:T(8,128)}) custom-call(s32[3]{0:T(128)S(1)} %add_add_fusion.1.info, f32[4]{0:T(128)S(1)} %copy-done.4, f32[4]{0:T(128)S(1)} %copy-done.5, ...), custom_call_target="tpu_custom_call", output_to_operand_aliasing={{0}: (9, {}), {1}: (10, {}), {2}: (11, {}), {3}: (12, {})} | custom-call | flops 4831838208 | bytes 6291456 | tf_op jit(solution)/shard_map/update/pallas_call | solution.py:373
  220.1 12.2 %mix.3 = bf16[2,256,2048]{2,1,0:T(8,128)(2,1)} custom-call(s32[3]{0:T(128)S(1)} %add_add_fusion.info, bf16[2,256,2048]{2,1,0:T(8,128)(2,1)S(1)} %copy-done.2, bf16[2,256,2048]{2,1,0:T(8,128)(2,1)S(1)} %copy-done.1, bf16[2,256,2048]{2,1,0:T(8,128)(2,1)} %values.7, bf16[2,256,2048]{2,1,0:T(8,128)(2,1)} %collective-permute-done.early_k, ...), custom_call_target="tpu_custom_call", output_to_operand_aliasing={{}: (8, {})} | custom-call | flops 2684354560 | bytes 18874368 | tf_op jit(solution)/shard_map/mix/pallas_call | solution.py:432
  232.3 0.5 collective-permute-start.19
  232.8 11.4 %update.13 = (f32[4,3,256,512]{3,2,1,0:T(8,128)}, f32[4,3,256,512]{3,2,1,0:T(8,128)}) custom-call(s32[3]{0:T(128)S(1)} %add_add_fusion.3.info, f32[4]{0:T(128)S(1)} %copy-done.4, f32[4]{0:T(128)S(1)} %copy-done.5, bf16[3,256,512]{2,1,0:T(8,128)(2,1)S(1)} %collective-permute-done.22.ga, ...), custom_call_target="tpu_custom_call", output_to_operand_aliasing={{0}: (9, {}), {1}: (10, {})} | custom-call | flops 4831838208 | bytes 6291456 | tf_op jit(solution)/shard_map/update/pallas_call | solution.py:373
  244.2 11.4 %update.14 = (f32[4,3,256,512]{3,2,1,0:T(8,128)}, f32[4,3,256,512]{3,2,1,0:T(8,128)}) custom-call(s32[3]{0:T(128)S(1)} %add_add_fusion.2.info, f32[4]{0:T(128)S(1)} %copy-done.4, f32[4]{0:T(128)S(1)} %copy-done.5, bf16[3,256,512]{2,1,0:T(8,128)(2,1)S(1)} %collective-permute-done.20.ga, ...), custom_call_target="tpu_custom_call", output_to_operand_aliasing={{0}: (9, {}), {1}: (10, {})} | custom-call | flops 4831838208 | bytes 6291456 | tf_op jit(solution)/shard_map/update/pallas_call | solution.py:373
  255.5 11.4 %update.15 = (f32[4,3,256,512]{3,2,1,0:T(8,128)}, f32[4,3,256,512]{3,2,1,0:T(8,128)}) custom-call(s32[3]{0:T(128)S(1)} %add_add_fusion.1.info, f32[4]{0:T(128)S(1)} %copy-done.4, f32[4]{0:T(128)S(1)} %copy-done.5, bf16[3,256,512]{2,1,0:T(8,128)(2,1)S(1)} %collective-permute-done.18.ga, ...), custom_call_target="tpu_custom_call", output_to_operand_aliasing={{0}: (9, {}), {1}: (10, {})} | custom-call | flops 4831838208 | bytes 6291456 | tf_op jit(solution)/shard_map/update/pallas_call | solution.py:373
  (41 shorter events, 0.1 us)
Async XLA Ops:
  0.6 33.4 %collective-permute-start.5 = (f32[4,3,256,512]{3,2,1,0:T(8,128)}, f32[4,3,256,512]{3,2,1,0:T(8,128)}, u32[]{:S(2)}, u32[]{:S(2)}) collective-permute-start(f32[4,3,256,512]{3,2,1,0:T(8,128)} %own.1), channel_id=1, source_target_pairs={{0,1},{1,0},{2,3},{3,2},{4,5},{5,4},{6,7},{7,6},{8,9},{9,8},{10,11... | collective-permute-start | bytes 18874376 | tf_op jit(solution)/shard_map/ppermute | solution.py:466
  1.1 45.9 %collective-permute-start.7 = (f32[4,3,256,512]{3,2,1,0:T(8,128)}, f32[4,3,256,512]{3,2,1,0:T(8,128)}, u32[]{:S(2)}, u32[]{:S(2)}) collective-permute-start(f32[4,3,256,512]{3,2,1,0:T(8,128)} %m_own.7), channel_id=1, source_target_pairs={{0,1},{1,0},{2,3},{3,2},{4,5},{5,4},{6,7},{7,6},{8,9},{9,8},{10,11... | collective-permute-start | bytes 18874376 | tf_op jit(solution)/shard_map/ppermute | solution.py:466
  2.2 1.6 copy-start
  6.1 15.7 %collective-permute-start.2 = (bf16[2,256,512]{2,1,0:T(8,128)(2,1)S(1)}, bf16[2,256,512]{2,1,0:T(8,128)(2,1)S(1)}, u32[]{:S(2)}, u32[]{:S(2)}) collective-permute-start(bf16[2,256,512]{2,1,0:T(8,128)(2,1)S(1)} %get-tuple-element.42), channel_id=1, source_target_pairs={{0,8},{8,0},{16,24},{24,16},{1,9},{9,1},{17,25},{25,17},{2,10},{10... | collective-permute-start | bytes 1572872 | tf_op jit(solution)/shard_map/ppermute | solution.py:463
  9.1 24.9 %collective-permute-start.3 = (bf16[2,256,512]{2,1,0:T(8,128)(2,1)S(1)}, bf16[2,256,512]{2,1,0:T(8,128)(2,1)S(1)}, u32[]{:S(2)}, u32[]{:S(2)}) collective-permute-start(bf16[2,256,512]{2,1,0:T(8,128)(2,1)S(1)} %get-tuple-element.43), channel_id=1, source_target_pairs={{0,16},{8,24},{16,0},{24,8},{1,17},{9,25},{17,1},{25,9},{2,18},{10... | collective-permute-start | bytes 1572872 | tf_op jit(solution)/shard_map/ppermute | solution.py:463
  10.6 23.3 %collective-permute-start.4 = (bf16[2,256,512]{2,1,0:T(8,128)(2,1)S(1)}, bf16[2,256,512]{2,1,0:T(8,128)(2,1)S(1)}, u32[]{:S(2)}, u32[]{:S(2)}) collective-permute-start(bf16[2,256,512]{2,1,0:T(8,128)(2,1)S(1)} %get-tuple-element.44), channel_id=1, source_target_pairs={{0,24},{8,16},{16,8},{24,0},{1,25},{9,17},{17,9},{25,1},{2,26},{10... | collective-permute-start | bytes 1572872 | tf_op jit(solution)/shard_map/ppermute | solution.py:463
  34.0 7.1 %copy-start.1 = (bf16[2,256,2048]{2,1,0:T(8,128)(2,1)S(1)}, bf16[2,256,2048]{2,1,0:T(8,128)(2,1)}, u32[]{:S(2)}) copy-start(bf16[2,256,2048]{2,1,0:T(8,128)(2,1)} %keys.7) | copy-start | bytes 6291460
  34.0 14.2 %copy-start.4 = (f32[4]{0:T(128)S(1)}, f32[4]{0:T(128)}, u32[]{:S(2)}) copy-start(f32[4]{0:T(128)} %rate.15) | copy-start | bytes 52
  34.0 14.2 %copy-start.5 = (f32[4]{0:T(128)S(1)}, f32[4]{0:T(128)}, u32[]{:S(2)}) copy-start(f32[4]{0:T(128)} %step.15) | copy-start | bytes 52
  41.0 6.1 %copy-start.3 = (bf16[2,3,256,512]{3,2,1,0:T(8,128)(2,1)}, bf16[2,3,256,512]{3,2,1,0:T(8,128)(2,1)S(1)}, u32[]{:S(2)}) copy-start(bf16[2,3,256,512]{3,2,1,0:T(8,128)(2,1)S(1)} %grad.2.ga) | copy-start | bytes 4718596
  41.0 6.0 %collective-permute-start.6 = (bf16[2,3,256,512]{3,2,1,0:T(8,128)(2,1)S(1)}, bf16[2,3,256,512]{3,2,1,0:T(8,128)(2,1)S(1)}, u32[]{:S(2)}, u32[]{:S(2)}) collective-permute-start(bf16[2,3,256,512]{3,2,1,0:T(8,128)(2,1)S(1)} %grad.2.ga), channel_id=1, source_target_pairs={{0,1},{1,0},{2,3},{3,2},{4,5},{5,4},{6,7},{7,6},{8,9},{9,8},{10,11... | collective-permute-start | bytes 4718600 | tf_op jit(solution)/shard_map/ppermute | solution.py:466
  43.5 20.9 %collective-permute-start.14 = (bf16[2,256,512]{2,1,0:T(8,128)(2,1)S(1)}, bf16[2,256,512]{2,1,0:T(8,128)(2,1)S(1)}, u32[]{:S(2)}, u32[]{:S(2)}) collective-permute-start(bf16[2,256,512]{2,1,0:T(8,128)(2,1)S(1)} %get-tuple-element.61), channel_id=1, source_target_pairs={{0,8},{8,0},{16,24},{24,16},{1,9},{9,1},{17,25},{25,17},{2,10},{10... | collective-permute-start | bytes 1572872 | tf_op jit(solution)/shard_map/ppermute | solution.py:463
  44.8 46.1 %collective-permute-start.15 = (bf16[2,256,512]{2,1,0:T(8,128)(2,1)S(1)}, bf16[2,256,512]{2,1,0:T(8,128)(2,1)S(1)}, u32[]{:S(2)}, u32[]{:S(2)}) collective-permute-start(bf16[2,256,512]{2,1,0:T(8,128)(2,1)S(1)} %get-tuple-element.62), channel_id=1, source_target_pairs={{0,16},{8,24},{16,0},{24,8},{1,17},{9,25},{17,1},{25,9},{2,18},{10... | collective-permute-start | bytes 1572872 | tf_op jit(solution)/shard_map/ppermute | solution.py:463
  45.6 45.3 %collective-permute-start.16 = (bf16[2,256,512]{2,1,0:T(8,128)(2,1)S(1)}, bf16[2,256,512]{2,1,0:T(8,128)(2,1)S(1)}, u32[]{:S(2)}, u32[]{:S(2)}) collective-permute-start(bf16[2,256,512]{2,1,0:T(8,128)(2,1)S(1)} %get-tuple-element.63), channel_id=1, source_target_pairs={{0,24},{8,16},{16,8},{24,0},{1,25},{9,17},{17,9},{25,1},{2,26},{10... | collective-permute-start | bytes 1572872 | tf_op jit(solution)/shard_map/ppermute | solution.py:463
  47.0 109.3 %collective-permute-start = (bf16[2,256,2048]{2,1,0:T(8,128)(2,1)S(1)}, bf16[2,256,2048]{2,1,0:T(8,128)(2,1)}, u32[]{:S(2)}, u32[]{:S(2)}) collective-permute-start(bf16[2,256,2048]{2,1,0:T(8,128)(2,1)S(1)} %copy-done.1), channel_id=1, source_target_pairs={{0,1},{1,8},{8,9},{9,16},{16,17},{17,24},{24,25},{25,0},{2,3},{3,1... | collective-permute-start | bytes 6291464 | tf_op jit(solution)/shard_map/ppermute | solution.py:26
  47.1 1.1 copy-start.10
  62.0 1.1 copy-start.6
  63.2 1.2 copy-start.8
  64.4 34.6 %copy-start.9 = (f32[1,3,256,512]{3,2,1,0:T(8,128)}, f32[1,3,256,512]{3,2,1,0:T(8,128)S(1)}, u32[]{:S(2)}) copy-start(f32[1,3,256,512]{3,2,1,0:T(8,128)S(1)} %get-tuple-element.64.refs_4_.w_own) | copy-start | bytes 4718596
  98.4 44.4 %collective-permute-start.17 = (bf16[2,3,256,512]{3,2,1,0:T(8,128)(2,1)}, bf16[2,3,256,512]{3,2,1,0:T(8,128)(2,1)}, u32[]{:S(2)}, u32[]{:S(2)}) collective-permute-start(bf16[2,3,256,512]{3,2,1,0:T(8,128)(2,1)} %grad.3.ga), channel_id=1, source_target_pairs={{0,1},{1,0},{2,3},{3,2},{4,5},{5,4},{6,7},{7,6},{8,9},{9,8},{10,11... | collective-permute-start | bytes 4718600 | tf_op jit(solution)/shard_map/ppermute | solution.py:466
  98.4 60.8 %collective-permute-start.1 = (bf16[2,256,2048]{2,1,0:T(8,128)(2,1)}, bf16[2,256,2048]{2,1,0:T(8,128)(2,1)}, u32[]{:S(2)}, u32[]{:S(2)}) collective-permute-start(bf16[2,256,2048]{2,1,0:T(8,128)(2,1)} %values.7), channel_id=1, source_target_pairs={{0,1},{1,8},{8,9},{9,16},{16,17},{17,24},{24,25},{25,0},{2,3},{3,1... | collective-permute-start | bytes 6291464 | tf_op jit(solution)/shard_map/ppermute | solution.py:26
  98.9 42.8 %collective-permute-start.10 = (bf16[3,256,512]{2,1,0:T(8,128)(2,1)}, bf16[3,256,512]{2,1,0:T(8,128)(2,1)S(1)}, u32[]{:S(2)}, u32[]{:S(2)}) collective-permute-start(bf16[3,256,512]{2,1,0:T(8,128)(2,1)} %get-tuple-element.45), channel_id=1, source_target_pairs={{0,16},{8,24},{16,0},{24,8},{1,17},{9,25},{17,1},{25,9},{2,18},{10... | collective-permute-start | bytes 2359304 | tf_op jit(solution)/shard_map/ppermute | solution.py:463
  101.4 40.4 %collective-permute-start.12 = (bf16[3,256,512]{2,1,0:T(8,128)(2,1)}, bf16[3,256,512]{2,1,0:T(8,128)(2,1)}, u32[]{:S(2)}, u32[]{:S(2)}) collective-permute-start(bf16[3,256,512]{2,1,0:T(8,128)(2,1)} %get-tuple-element.45), channel_id=1, source_target_pairs={{0,8},{8,0},{16,24},{24,16},{1,9},{9,1},{17,25},{25,17},{2,10},{10... | collective-permute-start | bytes 2359304 | tf_op jit(solution)/shard_map/ppermute | solution.py:463
  141.8 29.3 %collective-permute-start.8 = (bf16[3,256,512]{2,1,0:T(8,128)(2,1)}, bf16[3,256,512]{2,1,0:T(8,128)(2,1)S(1)}, u32[]{:S(2)}, u32[]{:S(2)}) collective-permute-start(bf16[3,256,512]{2,1,0:T(8,128)(2,1)} %get-tuple-element.45), channel_id=1, source_target_pairs={{0,24},{8,16},{16,8},{24,0},{1,25},{9,17},{17,9},{25,1},{2,26},{10... | collective-permute-start | bytes 2359304 | tf_op jit(solution)/shard_map/ppermute | solution.py:463
  141.8 43.2 %collective-permute-start.11 = (bf16[3,256,512]{2,1,0:T(8,128)(2,1)S(1)}, bf16[3,256,512]{2,1,0:T(8,128)(2,1)S(1)}, u32[]{:S(2)}, u32[]{:S(2)}) collective-permute-start(bf16[3,256,512]{2,1,0:T(8,128)(2,1)S(1)} %collective-permute-done.10.ga), channel_id=1, source_target_pairs={{0,1},{1,0},{2,3},{3,2},{4,5},{5,4},{6,7},{7,6},{8,9},{9,8},{10,11... | collective-permute-start | bytes 2359304 | tf_op jit(solution)/shard_map/ppermute | solution.py:466
  142.8 28.4 %collective-permute-start.13 = (bf16[3,256,512]{2,1,0:T(8,128)(2,1)}, bf16[3,256,512]{2,1,0:T(8,128)(2,1)S(1)}, u32[]{:S(2)}, u32[]{:S(2)}) collective-permute-start(bf16[3,256,512]{2,1,0:T(8,128)(2,1)} %collective-permute-done.12.ga), channel_id=1, source_target_pairs={{0,1},{1,0},{2,3},{3,2},{4,5},{5,4},{6,7},{7,6},{8,9},{9,8},{10,11... | collective-permute-start | bytes 2359304 | tf_op jit(solution)/shard_map/ppermute | solution.py:466
  142.8 1.4 copy-start.7
  144.2 14.9 %copy-start.2 = (bf16[2,256,2048]{2,1,0:T(8,128)(2,1)S(1)}, bf16[2,256,2048]{2,1,0:T(8,128)(2,1)}, u32[]{:S(2)}) copy-start(bf16[2,256,2048]{2,1,0:T(8,128)(2,1)} %queries.3) | copy-start | bytes 6291460
  156.3 28.6 %collective-permute-start.22 = (bf16[3,256,512]{2,1,0:T(8,128)(2,1)S(1)}, bf16[3,256,512]{2,1,0:T(8,128)(2,1)S(1)}, u32[]{:S(2)}, u32[]{:S(2)}) collective-permute-start(bf16[3,256,512]{2,1,0:T(8,128)(2,1)S(1)} %get-tuple-element.68), channel_id=1, source_target_pairs={{0,8},{8,0},{16,24},{24,16},{1,9},{9,1},{17,25},{25,17},{2,10},{10... | collective-permute-start | bytes 2359304 | tf_op jit(solution)/shard_map/ppermute | solution.py:463
  171.1 36.8 %collective-permute-start.9 = (bf16[3,256,512]{2,1,0:T(8,128)(2,1)S(1)}, bf16[3,256,512]{2,1,0:T(8,128)(2,1)S(1)}, u32[]{:S(2)}, u32[]{:S(2)}) collective-permute-start(bf16[3,256,512]{2,1,0:T(8,128)(2,1)S(1)} %collective-permute-done.8.ga), channel_id=1, source_target_pairs={{0,1},{1,0},{2,3},{3,2},{4,5},{5,4},{6,7},{7,6},{8,9},{9,8},{10,11... | collective-permute-start | bytes 2359304 | tf_op jit(solution)/shard_map/ppermute | solution.py:466
  171.1 61.2 %collective-permute-start.18 = (bf16[3,256,512]{2,1,0:T(8,128)(2,1)S(1)}, bf16[3,256,512]{2,1,0:T(8,128)(2,1)S(1)}, u32[]{:S(2)}, u32[]{:S(2)}) collective-permute-start(bf16[3,256,512]{2,1,0:T(8,128)(2,1)S(1)} %get-tuple-element.68), channel_id=1, source_target_pairs={{0,24},{8,16},{16,8},{24,0},{1,25},{9,17},{17,9},{25,1},{2,26},{10... | collective-permute-start | bytes 2359304 | tf_op jit(solution)/shard_map/ppermute | solution.py:463
  171.2 36.7 %collective-permute-start.20 = (bf16[3,256,512]{2,1,0:T(8,128)(2,1)S(1)}, bf16[3,256,512]{2,1,0:T(8,128)(2,1)S(1)}, u32[]{:S(2)}, u32[]{:S(2)}) collective-permute-start(bf16[3,256,512]{2,1,0:T(8,128)(2,1)S(1)} %get-tuple-element.68), channel_id=1, source_target_pairs={{0,16},{8,24},{16,0},{24,8},{1,17},{9,25},{17,1},{25,9},{2,18},{10... | collective-permute-start | bytes 2359304 | tf_op jit(solution)/shard_map/ppermute | solution.py:463
  184.9 47.9 %collective-permute-start.23 = (bf16[3,256,512]{2,1,0:T(8,128)(2,1)S(1)}, bf16[3,256,512]{2,1,0:T(8,128)(2,1)S(1)}, u32[]{:S(2)}, u32[]{:S(2)}) collective-permute-start(bf16[3,256,512]{2,1,0:T(8,128)(2,1)S(1)} %collective-permute-done.22.ga), channel_id=1, source_target_pairs={{0,1},{1,0},{2,3},{3,2},{4,5},{5,4},{6,7},{7,6},{8,9},{9,8},{10,11... | collective-permute-start | bytes 2359304 | tf_op jit(solution)/shard_map/ppermute | solution.py:466
  207.9 36.2 %collective-permute-start.21 = (bf16[3,256,512]{2,1,0:T(8,128)(2,1)S(1)}, bf16[3,256,512]{2,1,0:T(8,128)(2,1)S(1)}, u32[]{:S(2)}, u32[]{:S(2)}) collective-permute-start(bf16[3,256,512]{2,1,0:T(8,128)(2,1)S(1)} %collective-permute-done.20.ga), channel_id=1, source_target_pairs={{0,1},{1,0},{2,3},{3,2},{4,5},{5,4},{6,7},{7,6},{8,9},{9,8},{10,11... | collective-permute-start | bytes 2359304 | tf_op jit(solution)/shard_map/ppermute | solution.py:466
  232.3 23.2 %collective-permute-start.19 = (bf16[3,256,512]{2,1,0:T(8,128)(2,1)S(1)}, bf16[3,256,512]{2,1,0:T(8,128)(2,1)S(1)}, u32[]{:S(2)}, u32[]{:S(2)}) collective-permute-start(bf16[3,256,512]{2,1,0:T(8,128)(2,1)S(1)} %collective-permute-done.18.ga), channel_id=1, source_target_pairs={{0,1},{1,0},{2,3},{3,2},{4,5},{5,4},{6,7},{7,6},{8,9},{9,8},{10,11... | collective-permute-start | bytes 2359304 | tf_op jit(solution)/shard_map/ppermute | solution.py:466
